TPU v7x, 32 devices: a whole 2x2x4 slice. The times are simulated.
32 devices in a mesh: tm: 4 (over z), space: 8 (over y, x, core).
Axes of the slice: x: 2, y: 2, z: 4, core: 2. Of those that a mesh axis runs over, the one named last changes fastest.
Arguments:
- snaps: bfloat16 [4096, 3, 16384], P('tm', None, 'space')
- phase_bin: int32 [4096], P('tm'), may hold values from 0 to 15, as said below
- owner_order: int32 [16], replicated, may hold values from 0 to 15, each once
- modes: bfloat16 [16, 128, 3, 16384], P(None, None, None, 'space'), may hold values from -0.02734375 to 0.02734375
Outputs:
- phase_mean: bfloat16 [16, 3, 16384], P('tm', None, 'space')
- coefficients: float32 [4096, 128], P('tm')
Inputs may be any that keep to these rules, and one draw needn't show every extreme that they name: `phase_bin`: every bin is named by at least one snapshot; in each aligned block of 1024 snapshots no bin is named more than 128 times.
All inputs are finite; a program needn't handle non-finite values.
Results may differ from a plain program's by a relative error of at most 0.0068.
Values may be sent and summed in bfloat16 or wider, within the bound.
A program may use at most 192 MiB of HBM per device.

v0:
```python
import jax
import jax.numpy as jnp
from jax import lax
from jax.sharding import PartitionSpec as P


def on_device(snaps, phase_bin, owner_order, modes):
    snap_rows = snaps.shape[0]
    cell_count = snaps.shape[2]
    bin_total = modes.shape[0]
    mode_count = modes.shape[1]
    width = 3 * cell_count
    capacity = 2 * snap_rows // bin_total
    flattened = snaps.reshape(snap_rows, width)
    bin_ids = lax.broadcasted_iota(jnp.int32, (bin_total, 1), 0)
    matches = phase_bin[None, :] == bin_ids
    onehot = matches.astype(jnp.bfloat16)
    reorder = (owner_order[:, None] == bin_ids[:, 0][None, :]).astype(jnp.bfloat16)
    chosen = jnp.dot(reorder, onehot, preferred_element_type=jnp.float32)
    chosen_bf = chosen.astype(jnp.bfloat16)
    partial_sums = jnp.dot(chosen_bf, flattened, preferred_element_type=jnp.float32)
    partial_counts = jnp.sum(chosen, axis=1)
    total_sums, total_counts = lax.psum((partial_sums, partial_counts), "tm")
    all_mean = (total_sums / total_counts[:, None]).astype(jnp.bfloat16)
    own_rows = bin_total // lax.axis_size("tm")
    own_mean = lax.dynamic_slice_in_dim(all_mean, lax.axis_index("tm") * own_rows, own_rows, 0)
    phase_mean = own_mean.reshape(own_mean.shape[0], 3, cell_count)
    row_numbers = jnp.arange(bin_total, dtype=jnp.int32)
    inverse = jnp.zeros((bin_total,), jnp.int32).at[owner_order].set(row_numbers)
    mean_by_bin = jnp.take(all_mean, inverse, axis=0)
    match_int = matches.astype(jnp.int32)
    ranks = jnp.cumsum(match_int, axis=1) - 1
    slot = jnp.sum(match_int * ranks, axis=0)
    target = phase_bin * capacity + slot
    snap_numbers = jnp.arange(snap_rows, dtype=jnp.int32)
    source = jnp.full((bin_total * capacity,), snap_rows, jnp.int32).at[target].set(snap_numbers)
    gathered = jnp.take(flattened, source, axis=0, mode="fill", fill_value=0)
    gathered = gathered.reshape(bin_total, capacity, width)
    grouped = (gathered.astype(jnp.float32) - mean_by_bin.astype(jnp.float32)[:, None, :]).astype(
        jnp.bfloat16
    )
    modes_flat = modes.reshape(bin_total, mode_count, width)
    products = lax.dot_general(
        grouped, modes_flat, (((2,), (2,)), ((0,), (0,))), preferred_element_type=jnp.float32
    )
    picked = jnp.take(products.reshape(bin_total * capacity, mode_count), target, axis=0)
    coefficients = lax.psum(picked, "space")
    return (phase_mean, coefficients)


def solution(mesh):
    in_specs = (P("tm", None, "space"), P("tm"), P(), P(None, None, None, "space"))
    out_specs = (P("tm", None, "space"), P("tm", None))
    return jax.shard_map(
        on_device, mesh=mesh, in_specs=in_specs, out_specs=out_specs, check_vma=False
    )
```

profile of v0, /device:TPU:0, one launch (start us, length us, event | category | flops | bytes accessed | tf_op | source)
XLA Modules:
  0.0 239.0 jit_solution(14934051923834580583)
XLA Ops:
  7.2 0.0 copy-start
  7.2 0.0 copy-start.1
  7.2 0.0 all-reduce.3.cloned.1.call-start
  7.2 16.7 %copy.9 = bf16[1024,3,2048]{0,2,1:T(8,128)(2,1)} copy(bf16[1024,3,2048]{2,0,1:T(8,128)(2,1)} %param.4) | data formatting | bytes 25165824 | tf_op args[0]
  23.9 0.0 copy-done
  23.9 0.0 copy-done.1
  23.9 0.3 fusion.17
  24.2 8.7 %fusion.7 = f32[16,6144]{1,0:T(8,128)} fusion(bf16[1024,6144]{0,1:T(8,128)(2,1)} %bitcast.19, bf16[16,1024]{1,0:T(8,128)(2,1)S(1)} %get-tuple-element.5), kind=kOutput, calls=%fused_computation.19 | convolution fusion | flops 201326592 | bytes 13008896 | tf_op jit(solution)/shard_map/dot_general | solution.py:21
  32.9 0.0 all-reduce.3.cloned.1.call-update
  32.9 0.0 all-reduce.5.cloned.1.call-start
  33.0 16.7 %copy.12 = bf16[1024,6144]{1,0:T(8,128)(2,1)} copy(bf16[1024,6144]{0,1:T(8,128)(2,1)} %bitcast.20) | data formatting | bytes 25165824 | tf_op jit(solution)/shard_map/reshape | solution.py:14
  49.7 0.6 scatter_custom_fusion.1
  50.3 13.5 %psum.22 = f32[16]{0:T(128)S(1)} all-reduce(f32[16]{0:T(128)S(1)} %get-tuple-element.4), channel_id=1, replica_groups=mesh['tm'=4,'space'=8] {'tm'}, use_global_device_ids=true, to_apply=%region_2.0 | all-reduce | flops 16 | bytes 128 | tf_op jit(solution)/shard_map/psum | solution.py:23
  63.8 4.5 %reduce-window.6 = s32[16,8,128]{2,1,0:T(8,128)S(1)} reduce-window(s32[16,8,128]{2,1,0:T(8,128)S(1)} %fusion.5, s32[]{:T(128)} %constant.40.clone.1), window={size=1x1x128 pad=0_0x0_0x127_0}, to_apply=%region_3.0 | reduce-window | flops 2080768 | bytes 131076 | tf_op jit(solution)/shard_map/reduce-window
  68.4 0.1 slice.14
  68.4 0.1 copy.10
  68.6 0.1 copy.11
  68.7 0.1 select_reduce_fusion
  68.8 4.5 %scatter_custom_fusion = s32[2048]{0:T(1024)S(1)} fusion(s32[1024]{0:T(1024)S(1)} %get-tuple-element.3, s32[1024]{0:T(1024)S(1)} %iota.22, s32[]{:T(128)} %constant.65.clone.1), kind=kCustom, calls=%fused_computation.29 | custom fusion | bytes 8196 | tf_op jit(solution)/shard_map/scatter | solution.py:36
  73.3 32.6 %copy.13 = bf16[16,128,3,2048]{1,3,2,0:T(8,128)(2,1)} copy(bf16[16,128,3,2048]{3,1,2,0:T(8,128)(2,1)} %param.7) | data formatting | bytes 50331648 | tf_op args[3]
  106.0 48.0 %gather_fusion = bf16[2048,6144]{1,0:T(8,128)(2,1)} fusion(bf16[1024,6144]{1,0:T(8,128)(2,1)} %copy.12, s32[2048]{0:T(1024)S(1)} %fusion.10), kind=kCustom, calls=%fused_computation | custom fusion | bytes 50339840 | tf_op jit(solution)/shard_map/jit(_take)/gather | solution.py:37
  154.0 0.0 all-reduce.3.cloned.1.call-done
  154.0 1.1 divide_convert_fusion
  155.1 0.7 gather_fusion.1
  155.8 0.1 select_convert_fusion
  155.9 17.7 %fusion = f32[16,128,128]{2,1,0:T(8,128)S(1)} fusion(bf16[16,128,6144]{1,2,0:T(8,128)(2,1)} %bitcast.21, f32[16,6144]{1,0:T(8,128)S(1)} %select_convert_fusion, bf16[16,128,6144]{2,1,0:T(8,128)(2,1)} %bitcast.22, pred[16,128]{1,0:T(8,128)(4,1)S(1)} %and_bitcast_fusion), kind=kOutput, calls=%fused_computation.6 | convolution fusion | flops 3271557120 | bytes 51775488 | tf_op jit(solution)/shard_map/dot_general | solution.py:43
  173.6 2.8 %gather_fusion.2 = f32[1024,128]{1,0:T(8,128)S(1)} fusion(f32[2048,128]{1,0:T(8,128)S(1)} %bitcast.23, s32[1024]{0:T(1024)S(1)} %broadcast_clamp_fusion), kind=kCustom, calls=%fused_computation.2 | custom fusion | bytes 1052672 | tf_op jit(solution)/shard_map/jit(_take)/gather | solution.py:46
  176.4 1.0 broadcast_select_fusion
  177.4 0.0 all-reduce.5.cloned.1.call-update
  177.4 0.7 constant_dynamic-slice_fusion
  178.1 52.2 %all-reduce.5.cloned.1.call-done = f32[1024,128]{1,0:T(8,128)} async-done(((f32[1024,128]{1,0:T(8,128)}), f32[1024,128]{1,0:T(8,128)}) %all-reduce.5.cloned.1.call-update) | async-done | bytes 524304 | tf_op jit(solution)/shard_map/psum | solution.py:47
  230.3 1.9 copy.18
  (13 shorter events, 0.1 us)
Async XLA Ops:
  7.2 16.8 %copy-start = (s32[1024]{0:T(1024)S(1)}, s32[1024]{0:T(1024)}, u32[]{:S(2)}) copy-start(s32[1024]{0:T(1024)} %param.5) | copy-start | bytes 12292
  7.2 16.7 %copy-start.1 = (s32[16]{0:T(128)S(1)}, s32[16]{0:T(128)}, u32[]{:S(2)}) copy-start(s32[16]{0:T(128)} %param.6) | copy-start | bytes 196
  7.2 146.8 %all-reduce.3.cloned.1.call-start = ((), (), s32[]{:S(2)}) async-start(), calls=%async_computation | async-start | bytes 786432 | tf_op jit(solution)/shard_map/psum | solution.py:23
  32.9 197.3 %all-reduce.5.cloned.1.call-start = ((), (), s32[]{:S(2)}) async-start(), calls=%async_computation.1 | async-start | bytes 1048576 | tf_op jit(solution)/shard_map/psum | solution.py:47
Sparse Core Ops, SparseCore 0:
  33.1 39.8 all-reduce.2
  177.5 52.6 all-reduce.4
where the time goes:
time: 241 us; the launch traced here: 239 us
  local copies, waits for them, and re-layouts  125 us (52%)
  waiting for transfers between devices  52.2 us (22%)
  matrix products  26.7 us (11%)
  between operations  14.2 us (6%)
  blocking collectives  13.5 us (6%)
  other arithmetic  6.89 us (3%)
    psum x1, waiting for transfers between devices, on_device(): coefficients = lax.psum(picked, 'space')  52.2 us
    unnamed x7, local copies, waits for them, and re-layouts  51.2 us
    gather x1, local copies, waits for them, and re-layouts, on_device(): gathered = jnp.take(flattened, source, axis=0, mode='fill', fill_value=0)  48 us
    dot_general x1, matrix products, on_device(): lax.dot_general(grouped, modes_flat, (((2,), (2,)), ((0,), (0,))), prefer...  17.7 us
    reshape x1, local copies, waits for them, and re-layouts, on_device(): flattened = snaps.reshape(snap_rows, width)  16.7 us
    psum x1, blocking collectives, on_device(): total_sums, total_counts = lax.psum((partial_sums, partial_counts), 'tm')  13.5 us
    dot_general x1, matrix products, on_device(): jnp.dot(chosen_bf, flattened, preferred_element_type=jnp.float32)  8.7 us
  transfers between devices with their start and end apart: 2, of which 1 were waited for; matrix products, arithmetic and copies ran while one was open for 45% of the time, Pallas kernels for 0%

commit v1 on v0

--- a/solution.py
+++ b/solution.py
@@ -1,7 +1,21 @@
+import functools
 import jax
 import jax.numpy as jnp
 from jax import lax
 from jax.sharding import PartitionSpec as P
+
+
+def push_vector(mat, axis_id):
+    raw_out = mat
+    n_axis = lax.psum(1, axis_name=axis_id)
+    for dev_j in [
+        [(no, no ^ jj) for no in range(n_axis)] for jj in (1, 2, 4, 8, 16) if jj < n_axis
+    ]:
+        raw_out = raw_out + lax.ppermute(raw_out, axis_name=axis_id, perm=dev_j)
+    return raw_out
+
+
+edit_cards = functools.partial(push_vector, axis_id="space")
 
 
 def on_device(snaps, phase_bin, owner_order, modes):
@@ -44,7 +58,7 @@
         grouped, modes_flat, (((2,), (2,)), ((0,), (0,))), preferred_element_type=jnp.float32
     )
     picked = jnp.take(products.reshape(bin_total * capacity, mode_count), target, axis=0)
-    coefficients = lax.psum(picked, "space")
+    coefficients = edit_cards(picked)
     return (phase_mean, coefficients)
 
 

time: 241 us -> 215 us (0.89)
  waiting for transfers between devices: 52.2 us -> 25.2 us
  starting transfers between devices: 0.08 us -> 3.44 us
    psum x1 -> x0, waiting for transfers between devices: 52.2 us -> none  [on_device(): coefficients = lax.psum(picked, 'space')]
    ppermute x0 -> x3, waiting for transfers between devices: none -> 25.1 us  [push_vector(): raw_out = raw_out + lax.ppermute(raw_out, axis_name=axis_id, perm=dev_j)]
    ppermute x0 -> x3, starting transfers between devices: none -> 3.4 us  [push_vector(): raw_out = raw_out + lax.ppermute(raw_out, axis_name=axis_id, perm=dev_j)]
    unnamed x7 -> x6, local copies, waits for them, and re-layouts: 51.2 us -> 49.3 us
  transfers between devices with their start and end apart: 2 -> 4, of which waited for: 1 -> 3; matrix products, arithmetic and copies ran while one was open for 45% -> 51% of each run, Pallas kernels for 0% -> 0%
where the time goes in v1:
time: 215 us; the launch traced here: 214 us
  local copies, waits for them, and re-layouts  124 us (58%)
  matrix products  26.7 us (12%)
  waiting for transfers between devices  25.2 us (12%)
  between operations  14.2 us (7%)
  blocking collectives  13.4 us (6%)
  other arithmetic  7.19 us (3%)
  starting transfers between devices  3.44 us (2%)
    unnamed x6, local copies, waits for them, and re-layouts  49.3 us
    gather x1, local copies, waits for them, and re-layouts, on_device(): gathered = jnp.take(flattened, source, axis=0, mode='fill', fill_value=0)  48 us
    ppermute x3, waiting for transfers between devices, push_vector(): raw_out = raw_out + lax.ppermute(raw_out, axis_name=axis_id, perm=dev_j)  25.1 us
    dot_general x1, matrix products, on_device(): lax.dot_general(grouped, modes_flat, (((2,), (2,)), ((0,), (0,))), prefer...  17.7 us
    reshape x1, local copies, waits for them, and re-layouts, on_device(): flattened = snaps.reshape(snap_rows, width)  16.7 us
    psum x1, blocking collectives, on_device(): total_sums, total_counts = lax.psum((partial_sums, partial_counts), 'tm')  13.4 us
    dot_general x1, matrix products, on_device(): jnp.dot(chosen_bf, flattened, preferred_element_type=jnp.float32)  8.7 us
    another operation x2, other arithmetic  4.55 us
  transfers between devices with their start and end apart: 4, of which 3 were waited for; matrix products, arithmetic and copies ran while one was open for 51% of the time, Pallas kernels for 0%

profile of v1, /device:TPU:0, one launch (start us, length us, event | category | flops | bytes accessed | tf_op | source)
XLA Modules:
  0.0 213.6 jit_solution(15479498690608505950)
XLA Ops:
  7.2 0.0 copy-start
  7.2 0.0 copy-start.1
  7.2 0.0 all-reduce.2.cloned.1.call-start
  7.2 16.7 %copy.9 = bf16[1024,3,2048]{0,2,1:T(8,128)(2,1)} copy(bf16[1024,3,2048]{2,0,1:T(8,128)(2,1)} %param.4) | data formatting | bytes 25165824 | tf_op args[0]
  23.9 0.0 copy-done
  23.9 0.0 copy-done.1
  23.9 0.3 fusion.17
  24.2 8.7 %fusion.7 = f32[16,6144]{1,0:T(8,128)} fusion(bf16[1024,6144]{0,1:T(8,128)(2,1)} %bitcast.19, bf16[16,1024]{1,0:T(8,128)(2,1)S(1)} %get-tuple-element.5), kind=kOutput, calls=%fused_computation.19 | convolution fusion | flops 201326592 | bytes 13008896 | tf_op jit(solution)/shard_map/dot_general | solution.py:35
  32.9 0.0 all-reduce.2.cloned.1.call-update
  33.0 16.7 %copy.12 = bf16[1024,6144]{1,0:T(8,128)(2,1)} copy(bf16[1024,6144]{0,1:T(8,128)(2,1)} %bitcast.20) | data formatting | bytes 25165824 | tf_op jit(solution)/shard_map/reshape | solution.py:28
  49.6 0.6 scatter_custom_fusion.1
  50.3 13.4 %psum.15 = f32[16]{0:T(128)S(1)} all-reduce(f32[16]{0:T(128)S(1)} %get-tuple-element.4), channel_id=1, replica_groups=mesh['tm'=4,'space'=8] {'tm'}, use_global_device_ids=true, to_apply=%region_2.0 | all-reduce | flops 16 | bytes 128 | tf_op jit(solution)/shard_map/psum | solution.py:37
  63.7 4.5 %reduce-window.6 = s32[16,8,128]{2,1,0:T(8,128)S(1)} reduce-window(s32[16,8,128]{2,1,0:T(8,128)S(1)} %fusion.5, s32[]{:T(128)} %constant.40.clone.1), window={size=1x1x128 pad=0_0x0_0x127_0}, to_apply=%region_3.0 | reduce-window | flops 2080768 | bytes 131076 | tf_op jit(solution)/shard_map/reduce-window
  68.2 0.1 slice.14
  68.3 0.1 copy.10
  68.5 0.1 copy.11
  68.5 0.1 select_reduce_fusion
  68.7 4.5 %scatter_custom_fusion = s32[2048]{0:T(1024)S(1)} fusion(s32[1024]{0:T(1024)S(1)} %get-tuple-element.3, s32[1024]{0:T(1024)S(1)} %iota.22, s32[]{:T(128)} %constant.65.clone.1), kind=kCustom, calls=%fused_computation.29 | custom fusion | bytes 8196 | tf_op jit(solution)/shard_map/scatter | solution.py:50
  73.2 32.6 %copy.13 = bf16[16,128,3,2048]{1,3,2,0:T(8,128)(2,1)} copy(bf16[16,128,3,2048]{3,1,2,0:T(8,128)(2,1)} %param.7) | data formatting | bytes 50331648 | tf_op args[3]
  105.8 48.0 %gather_fusion = bf16[2048,6144]{1,0:T(8,128)(2,1)} fusion(bf16[1024,6144]{1,0:T(8,128)(2,1)} %copy.12, s32[2048]{0:T(1024)S(1)} %fusion.10), kind=kCustom, calls=%fused_computation | custom fusion | bytes 50339840 | tf_op jit(solution)/shard_map/jit(_take)/gather | solution.py:51
  153.8 0.0 all-reduce.2.cloned.1.call-done
  153.9 1.1 divide_convert_fusion
  154.9 0.7 gather_fusion.1
  155.6 0.1 select_convert_fusion
  155.7 17.7 %fusion = f32[16,128,128]{2,1,0:T(8,128)S(1)} fusion(bf16[16,128,6144]{1,2,0:T(8,128)(2,1)} %bitcast.21, f32[16,6144]{1,0:T(8,128)S(1)} %select_convert_fusion, bf16[16,128,6144]{2,1,0:T(8,128)(2,1)} %bitcast.22, pred[16,128]{1,0:T(8,128)(4,1)S(1)} %and_bitcast_fusion), kind=kOutput, calls=%fused_computation.6 | convolution fusion | flops 3271557120 | bytes 51775488 | tf_op jit(solution)/shard_map/dot_general | solution.py:57
  173.4 2.8 %gather_fusion.2 = f32[1024,128]{1,0:T(8,128)S(1)} fusion(f32[2048,128]{1,0:T(8,128)S(1)} %bitcast.23, s32[1024]{0:T(1024)S(1)} %broadcast_clamp_fusion), kind=kCustom, calls=%fused_computation.2 | custom fusion | bytes 1052672 | tf_op jit(solution)/shard_map/jit(_take)/gather | solution.py:60
  176.2 0.2 broadcast_select_fusion
  176.5 0.1 collective-permute-start
  176.5 1.9 collective-permute-done
  178.4 0.2 fusion.21
  178.6 1.7 collective-permute-start.1
  180.3 12.4 %collective-permute-done.1 = f32[1024,128]{1,0:T(8,128)S(1)} collective-permute-done((f32[1024,128]{1,0:T(8,128)S(1)}, f32[1024,128]{1,0:T(8,128)S(1)}, u32[]{:S(2)}, u32[]{:S(2)}) %collective-permute-start.1) | collective-permute-done | bytes 524320 | tf_op jit(solution)/shard_map/ppermute | solution.py:14
  192.7 0.1 add.52
  192.7 1.7 collective-permute-start.2
  194.4 0.6 constant_dynamic-slice_fusion
  195.1 10.9 %collective-permute-done.2 = f32[1024,128]{1,0:T(8,128)S(1)} collective-permute-done((f32[1024,128]{1,0:T(8,128)S(1)}, f32[1024,128]{1,0:T(8,128)S(1)}, u32[]{:S(2)}, u32[]{:S(2)}) %collective-permute-start.2) | collective-permute-done | bytes 524320 | tf_op jit(solution)/shard_map/ppermute | solution.py:14
  205.9 0.8 add.53
  (13 shorter events, 0.1 us)
Async XLA Ops:
  7.2 16.8 %copy-start = (s32[1024]{0:T(1024)S(1)}, s32[1024]{0:T(1024)}, u32[]{:S(2)}) copy-start(s32[1024]{0:T(1024)} %param.5) | copy-start | bytes 12292
  7.2 16.7 %copy-start.1 = (s32[16]{0:T(128)S(1)}, s32[16]{0:T(128)}, u32[]{:S(2)}) copy-start(s32[16]{0:T(128)} %param.6) | copy-start | bytes 196
  7.2 146.7 %all-reduce.2.cloned.1.call-start = ((), (), s32[]{:S(2)}) async-start(), calls=%async_computation | async-start | bytes 786432 | tf_op jit(solution)/shard_map/psum | solution.py:37
  176.5 2.0 collective-permute-start
  178.6 14.0 %collective-permute-start.1 = (f32[1024,128]{1,0:T(8,128)S(1)}, f32[1024,128]{1,0:T(8,128)S(1)}, u32[]{:S(2)}, u32[]{:S(2)}) collective-permute-start(f32[1024,128]{1,0:T(8,128)S(1)} %fusion.21), channel_id=1, source_target_pairs={{0,2},{1,3},{2,0},{3,1},{4,6},{5,7},{6,4},{7,5},{8,10},{9,11},{10,... | collective-permute-start | bytes 1572872 | tf_op jit(solution)/shard_map/ppermute | solution.py:14
  192.7 13.2 %collective-permute-start.2 = (f32[1024,128]{1,0:T(8,128)S(1)}, f32[1024,128]{1,0:T(8,128)S(1)}, u32[]{:S(2)}, u32[]{:S(2)}) collective-permute-start(f32[1024,128]{1,0:T(8,128)S(1)} %add.52), channel_id=1, source_target_pairs={{0,4},{1,5},{2,6},{3,7},{4,0},{5,1},{6,2},{7,3},{8,12},{9,13},{10,... | collective-permute-start | bytes 1572872 | tf_op jit(solution)/shard_map/ppermute | solution.py:14
Sparse Core Ops, SparseCore 0:
  33.1 39.7 all-reduce.1
